TPU v7x, 128 devices: a whole 4x4x4 slice. The times are simulated.
128 devices in a mesh: batch: 32 (over z, x, core), hidden: 4 (over y).
Axes of the slice: x: 4, y: 4, z: 4, core: 2. Of those that a mesh axis runs over, the one named last changes fastest.
Arguments:
- tables: float32 [26, 131072, 16], P(None, ('batch', 'hidden')), may hold values from -6 to 6
- dense: float32 [16384, 13], P('batch'), may hold values from -6 to 6
- dense_weight: float32 [13, 96], replicated, may hold values from -1.75 to 1.75
- expert_in: float32 [512, 8, 256], P(None, None, 'hidden'), may hold values from -0.25 to 0.25
- expert_out: float32 [8, 256, 128], P(None, 'hidden'), may hold values from -0.375 to 0.375
- gate_weight: float32 [2, 512, 8], replicated, may hold values from -0.125 to 0.125
- tower_weight: float32 [2, 128, 64], replicated, may hold values from -0.5 to 0.5
- head_weight: float32 [2, 64], replicated, may hold values from -0.75 to 0.75
- slots: int32 [16384, 26], P('batch'), may hold values from 0 to 4095, as said below
- requests: int32 [32, 128, 32], P('batch'), may hold values from 0 to 26623
- pred_cot: float32 [16384, 2], P(('batch', 'hidden')), may hold values from -6 to 6
Outputs:
- predictions: float32 [16384, 2], P(('batch', 'hidden'))
- dense_grad: float32 [16384, 13], P('batch')
- table_grad: float32 [26, 131072, 16], P(None, ('batch', 'hidden'))
- dense_weight_grad: float32 [13, 96], replicated
- expert_in_grad: float32 [512, 8, 256], P(None, None, 'hidden')
- expert_out_grad: float32 [8, 256, 128], P(None, 'hidden')
- gate_grad: float32 [2, 512, 8], replicated
- tower_grad: float32 [2, 128, 64], replicated
- head_grad: float32 [2, 64], replicated
Inputs may be any that keep to these rules, and one draw needn't show every extreme that they name: slots[e, t] = o * 32 + j names slot j of owner o in the fetch list of the example's group; in every group some owner has all 32 slots named, and every owner is named. requests[g, o, j] = v names row o * 1024 + (v mod 1024) of table floor(v / 1024).
All inputs are finite; a program needn't handle non-finite values.
Results may differ from a plain program's by a relative error of at most 0.0003.
Values sent between devices are 32-bit elements; how exact they have to be, the bound alone decides.
A program may use at most 64 MiB of HBM per device.

v0:
```python
import jax
import jax.numpy as jnp
from jax import lax
from jax.sharding import PartitionSpec as P

highest = lax.Precision.HIGHEST


def silu_both(value):
    sigma = jax.nn.sigmoid(value)
    return (value * sigma, sigma * (1.0 + value * (1.0 - sigma)))


def tower_pass(rows_in, expert_pre, cotangent, weights_row, gate_weight, tower_weight, head_weight):
    expert_outputs, expert_slope = silu_both(expert_pre)
    logits = jnp.einsum("nd,tde->nte", rows_in, gate_weight, precision=highest)
    gates = jax.nn.softmax(logits, axis=-1)
    mixed = jnp.einsum("nte,neo->nto", gates, expert_outputs, precision=highest)
    tower_pre = jnp.einsum("nto,tow->ntw", mixed, tower_weight, precision=highest)
    towers, tower_slope = silu_both(tower_pre)
    predicted = jax.nn.sigmoid(jnp.einsum("ntw,tw->nt", towers, head_weight, precision=highest))
    score_grad = cotangent * predicted * (1.0 - predicted)
    head_grad = jnp.einsum("ntw,nt->tw", towers, score_grad * weights_row, precision=highest)
    tower_pre_grad = score_grad[:, :, None] * head_weight[None] * tower_slope
    tower_grad = jnp.einsum(
        "nto,ntw->tow", mixed, tower_pre_grad * weights_row[:, :, None], precision=highest
    )
    mixed_grad = jnp.einsum("ntw,tow->nto", tower_pre_grad, tower_weight, precision=highest)
    gate_slope = jnp.einsum("nto,neo->nte", mixed_grad, expert_outputs, precision=highest)
    logit_grad = gates * (gate_slope - jnp.sum(gates * gate_slope, axis=-1, keepdims=True))
    gate_grad = jnp.einsum(
        "nd,nte->tde", rows_in, logit_grad * weights_row[:, :, None], precision=highest
    )
    input_part = jnp.einsum("nte,tde->nd", logit_grad, gate_weight, precision=highest)
    expert_pre_grad = (
        jnp.einsum("nte,nto->neo", gates, mixed_grad, precision=highest) * expert_slope
    )
    return (predicted, expert_pre_grad, input_part, gate_grad, tower_grad, head_grad)


def on_device(
    tables,
    dense,
    dense_weight,
    expert_in,
    expert_out,
    gate_weight,
    tower_weight,
    head_weight,
    slots,
    requests,
    pred_cot,
):
    hidden_count = lax.axis_size("hidden")
    my_index = lax.axis_index("hidden")
    table_count, table_rows, entry_width = tables.shape
    table_flat = tables.reshape(table_count * table_rows, entry_width)
    owner_count = requests.shape[1]
    capacity = requests.shape[2]
    portion = capacity // hidden_count
    asked = requests[0]
    all_ids = lax.all_to_all(asked, ("batch", "hidden"), split_axis=0, concat_axis=0, tiled=True)
    found_rows = jnp.take(table_flat, all_ids.reshape(-1), axis=0).reshape(
        owner_count, capacity * entry_width
    )
    fetched = lax.all_to_all(
        found_rows, ("batch", "hidden"), split_axis=0, concat_axis=0, tiled=True
    )
    blocks = all_ids.reshape(owner_count // hidden_count, hidden_count, hidden_count, portion)
    diagonal = jnp.arange(hidden_count)
    kept_ids = blocks[:, diagonal, diagonal, :].reshape(owner_count, portion)
    examples = slots.shape[0]
    embed_width = slots.shape[1] * entry_width
    flat_slots = slots.reshape(-1)
    embed = jnp.take(fetched.reshape(owner_count * capacity, entry_width), flat_slots, axis=0)
    projected = jnp.dot(dense, dense_weight, precision=highest)
    features = jnp.concatenate([embed.reshape(examples, embed_width), projected], axis=1)
    model_width = features.shape[1]
    expert_count = expert_in.shape[1]
    inner_width = expert_in.shape[2]
    flat_in = expert_in.reshape(model_width, expert_count * inner_width)
    inner_pre = jnp.dot(features, flat_in, precision=highest).reshape(
        examples, expert_count, inner_width
    )
    inner, inner_slope = silu_both(inner_pre)
    quarter = examples // hidden_count
    start_row = my_index * quarter
    expert_pre = lax.psum_scatter(
        jnp.einsum("nek,eko->neo", inner, expert_out, precision=highest),
        "hidden",
        scatter_dimension=0,
        tiled=True,
    )
    rows_in = lax.dynamic_slice_in_dim(features, start_row, quarter, 0)
    predictions, local_pre_grad, input_part, gate_grad, tower_grad, head_grad = tower_pass(
        rows_in,
        expert_pre,
        pred_cot,
        jnp.ones((quarter, 1), jnp.float32),
        gate_weight,
        tower_weight,
        head_weight,
    )
    expert_pre_grad = lax.all_gather(local_pre_grad, "hidden", axis=0, tiled=True)
    gate_input = lax.dynamic_update_slice_in_dim(
        jnp.zeros((examples, model_width), jnp.float32), input_part, start_row, 0
    )
    out_grad = jnp.einsum("nek,neo->eko", inner, expert_pre_grad, precision=highest)
    inner_grad = (
        jnp.einsum("neo,eko->nek", expert_pre_grad, expert_out, precision=highest) * inner_slope
    )
    flat_inner_grad = inner_grad.reshape(examples, expert_count * inner_width)
    in_grad = jnp.dot(features.T, flat_inner_grad, precision=highest).reshape(expert_in.shape)
    feature_part = jnp.dot(flat_inner_grad, flat_in.T, precision=highest) + gate_input
    feature_grad = lax.psum(feature_part, "hidden")
    projected_grad = feature_grad[:, embed_width:]
    dense_grad = jnp.dot(projected_grad, dense_weight.T, precision=highest)
    dense_rows = lax.dynamic_slice_in_dim(dense, start_row, quarter, 0)
    projected_rows = lax.dynamic_slice_in_dim(projected_grad, start_row, quarter, 0)
    dense_weight_grad = jnp.dot(dense_rows.T, projected_rows, precision=highest)
    embed_grad = feature_grad[:, :embed_width].reshape(examples * slots.shape[1], entry_width)
    slot_grad = (
        jnp.zeros((owner_count * capacity, entry_width), jnp.float32).at[flat_slots].add(embed_grad)
    )
    slot_grad = slot_grad.reshape(owner_count, capacity * entry_width)
    my_grad = lax.dynamic_slice_in_dim(
        slot_grad, my_index * portion * entry_width, portion * entry_width, 1
    )
    returned = lax.all_to_all(my_grad, ("batch", "hidden"), split_axis=0, concat_axis=0, tiled=True)
    table_grad = (
        jnp.zeros_like(table_flat).at[kept_ids.reshape(-1)].add(returned.reshape(-1, entry_width))
    )
    table_grad = table_grad.reshape(tables.shape)
    in_grad, out_grad = lax.psum((in_grad, out_grad), "batch")
    dense_weight_grad, gate_grad, tower_grad, head_grad = lax.psum(
        (dense_weight_grad, gate_grad, tower_grad, head_grad), ("batch", "hidden")
    )
    return (
        predictions,
        dense_grad,
        table_grad,
        dense_weight_grad,
        in_grad,
        out_grad,
        gate_grad,
        tower_grad,
        head_grad,
    )


def solution(mesh):
    placed = (
        P(None, ("batch", "hidden"), None),
        P("batch", None),
        P(),
        P(None, None, "hidden"),
        P(None, "hidden", None),
        P(),
        P(),
        P(),
        P("batch", None),
        P("batch", None, None),
        P(("batch", "hidden"), None),
    )
    return jax.shard_map(
        on_device,
        mesh=mesh,
        in_specs=placed,
        out_specs=(
            P(("batch", "hidden"), None),
            P("batch", None),
            P(None, ("batch", "hidden"), None),
            P(),
            P(None, None, "hidden"),
            P(None, "hidden", None),
            P(),
            P(),
            P(),
        ),
        check_vma=False,
    )
```

profile of v0, /device:TPU:1, one launch (start us, length us, event | category | flops | bytes accessed | tf_op | source)
XLA Modules:
  0.0 512.1 jit_solution(7730485191456762924)
XLA Ops:
  8.7 11.5 %all-to-all-start = ((s32[128,1,32]{2,1,0:T(1,128)}), s32[128,1,32]{2,1,0:T(1,128)S(1)}, u32[]{:S(2)}, u32[]{:S(2)}) async-start(s32[128,1,32]{2,1,0:T(1,128)} %bitcast.1), calls=%async_computation | async-start | bytes 131072 | tf_op jit(solution)/shard_map/all_to_all | solution.py:62
  21.6 8.5 %copy.82 = f32[26,1024,16]{2,1,0:T(8,128)} copy(f32[26,1024,16]{1,2,0:T(8,128)} %param.11) | data formatting | bytes 3407872 | tf_op args[0]
  31.6 15.6 %gather_fusion = f32[4096,16]{1,0:T(8,128)S(1)} fusion(f32[26624,16]{1,0:T(8,128)} %bitcast.95, s32[4096]{0:T(1024)S(1)} %broadcast_clamp_fusion.1), kind=kCustom, calls=%fused_computation | custom fusion | bytes 540672 | tf_op jit(solution)/shard_map/jit(_take)/gather | solution.py:63
  49.9 9.8 %all-to-all-start.1 = ((f32[128,1,512]{2,1,0:T(1,128)}), f32[128,1,512]{2,1,0:T(1,128)S(1)}, u32[]{:S(2)}, u32[]{:S(2)}) async-start(f32[128,1,512]{2,1,0:T(1,128)} %copy.84), calls=%async_computation.1 | async-start | bytes 524288 | tf_op jit(solution)/shard_map/all_to_all | solution.py:66
  62.0 8.8 %all-to-all-done.1 = f32[128,1,512]{2,1,0:T(1,128)S(1)} async-done(((f32[128,1,512]{2,1,0:T(1,128)}), f32[128,1,512]{2,1,0:T(1,128)S(1)}, u32[]{:S(2)}, u32[]{:S(2)}) %all-to-all-start.1) | async-done | bytes 262176 | tf_op jit(solution)/shard_map/all_to_all | solution.py:66
  73.9 44.6 %gather_fusion.1 = f32[13312,16]{1,0:T(8,128)} fusion(f32[4096,16]{1,0:T(8,128)S(1)} %reshape.199, s32[13312]{0:T(1024)S(1)} %broadcast_clamp_fusion), kind=kCustom, calls=%fused_computation.1 | custom fusion | bytes 1757184 | tf_op jit(solution)/shard_map/jit(_take)/gather | solution.py:75
  118.5 4.4 gather.18
  126.0 4.8 convolution_bitcast_fusion
  132.7 23.8 %reduce-scatter.2.cloned.1.call-done = f32[128,8,128]{2,0,1:T(8,128)} async-done(((f32[512,8,128]{2,0,1:T(8,128)}), f32[128,8,128]{2,0,1:T(8,128)}) %reduce-scatter.2.cloned.1.call-update) | async-done | bytes 524304 | tf_op jit(solution)/shard_map/reduce_scatter | solution.py:88
  166.6 2.2 fusion.19
  169.6 27.6 %all-gather.2.cloned.1.call-done = f32[512,8,128]{2,0,1:T(8,128)} async-done(((f32[128,8,128]{2,0,1:T(8,128)}), f32[512,8,128]{2,0,1:T(8,128)}) %all-gather.2.cloned.1.call-update) | async-done | bytes 2097168 | tf_op jit(solution)/shard_map/all_gather | solution.py:104
  197.2 4.4 fusion.3
  210.4 4.2 fusion.25
  214.6 2.9 fusion.9
  217.8 32.7 %all-reduce.6.cloned.1.call-done = f32[512,512]{1,0:T(8,128)} async-done(((f32[512,512]{1,0:T(8,128)}), f32[512,512]{1,0:T(8,128)}) %all-reduce.6.cloned.1.call-update) | async-done | bytes 1048592 | tf_op jit(solution)/shard_map/psum | solution.py:115
  250.5 5.6 %reshape.234 = f32[13312,16]{1,0:T(8,128)} reshape(f32[512,416]{1,0:T(8,128)} %bitcast.97) | data formatting | bytes 1703936 | tf_op jit(solution)/shard_map/reshape | solution.py:121
  256.1 71.9 %scatter_custom_fusion = f32[4096,16]{1,0:T(8,128)S(1)} fusion(s32[13312]{0:T(1024)} %bitcast.104, f32[13312,16]{1,0:T(8,128)} %reshape.234, f32[]{:T(128)} %constant.26.clone.1), kind=kCustom, calls=%fused_computation.28 | custom fusion | flops 212992 | bytes 262656 | tf_op jit(solution)/shard_map/scatter-add | solution.py:123
  330.2 10.5 %all-to-all-start.2 = ((f32[128,1,128]{2,1,0:T(1,128)}), f32[128,1,128]{2,1,0:T(1,128)S(1)}, u32[]{:S(2)}, u32[]{:S(2)}) async-start(f32[128,1,128]{2,1,0:T(1,128)} %bitcast.28), calls=%async_computation.3 | async-start | bytes 131072 | tf_op jit(solution)/shard_map/all_to_all | solution.py:129
  341.8 2.0 fusion.50
  344.7 68.5 %all-reduce = (f32[13,96]{1,0:T(8,128)}, f32[2,512,8]{1,2,0:T(8,128)}, f32[2,64]{1,0:T(2,128)}) all-reduce(f32[13,96]{1,0:T(8,128)S(1)} %fusion.34, f32[2,512,8]{1,2,0:T(8,128)S(1)} %convolution_bitcast_fusion.6, f32[2,64]{1,0:T(2,128)S(1)} %bitcast.109), channel_id=1, replica_groups=mesh['batch'=32,'hidden'=4] {'batch','hidden'}, use_global_device_ids=true, to_apply=%region_7.8 | all-reduce | flops 9568 | bytes 76544 | tf_op jit(solution)/shard_map/psum | solution.py:135
  414.7 11.8 %scatter_custom_fusion.1 = f32[26624,16]{1,0:T(8,128)} fusion(s32[1024]{0:T(1024)S(1)} %bitcast.106, f32[1024,16]{1,0:T(8,128)S(1)} %reshape.242, f32[]{:T(128)} %constant.26.clone.1), kind=kCustom, calls=%fused_computation.6 | custom fusion | flops 16384 | bytes 1703940 | tf_op jit(solution)/shard_map/scatter-add | solution.py:131
  426.4 8.9 %copy.102 = f32[26,1024,16]{1,2,0:T(8,128)} copy(f32[26,1024,16]{2,1,0:T(8,128)} %bitcast.96) | data formatting | bytes 3407872
  435.3 66.3 %all-reduce.10.cloned.1.call-done = (f32[512,8,64]{0,2,1:T(8,128)}, f32[8,64,128]{2,1,0:T(8,128)}) async-done(((f32[512,8,64]{0,2,1:T(8,128)}, f32[8,64,128]{2,1,0:T(8,128)}), (f32[512,8,64]{0,2,1:T(8,128)}, f32[8,64,128]{2,1,0:T(8,128)})) %all-reduce.10.cloned.1.call-update) | async-done | bytes 1310736 | tf_op jit(solution)/shard_map/psum | solution.py:134
  501.6 2.3 copy.128
  (123 shorter events, 43.9 us)
Async XLA Ops:
  7.2 116.9 %copy-start = (f32[512,8,64]{0,2,1:T(8,128)S(1)}, f32[512,8,64]{0,2,1:T(8,128)}, u32[]{:S(2)}) copy-start(f32[512,8,64]{0,2,1:T(8,128)} %param.14) | copy-start | bytes 3145732
  8.7 21.3 %all-to-all-start = ((s32[128,1,32]{2,1,0:T(1,128)}), s32[128,1,32]{2,1,0:T(1,128)S(1)}, u32[]{:S(2)}, u32[]{:S(2)}) async-start(s32[128,1,32]{2,1,0:T(1,128)} %bitcast.1), calls=%async_computation | async-start | bytes 131072 | tf_op jit(solution)/shard_map/all_to_all | solution.py:62
  21.5 8.5 %copy-start.12 = (s32[13312,1]{0,1:T(1,128)}, s32[13312,1]{0,1:T(1,128)S(1)}, u32[]{:S(2)}) copy-start(s32[13312,1]{0,1:T(1,128)S(1)} %compare_select_fusion) | copy-start | bytes 159748
  47.3 12.9 %copy-start.10 = (s32[512,26]{0,1:T(8,128)S(1)}, s32[512,26]{0,1:T(8,128)}, u32[]{:S(2)}) copy-start(s32[512,26]{0,1:T(8,128)} %param.19) | copy-start | bytes 159748
  48.9 12.5 %copy-start.17 = (f32[512,13]{0,1:T(8,128)S(1)}, f32[512,13]{0,1:T(8,128)}, u32[]{:S(2)}) copy-start(f32[512,13]{0,1:T(8,128)} %param.12) | copy-start | bytes 79876
  48.9 12.5 %copy-start.18 = (f32[13,96]{1,0:T(8,128)S(1)}, f32[13,96]{1,0:T(8,128)}, u32[]{:S(2)}) copy-start(f32[13,96]{1,0:T(8,128)} %param.13) | copy-start | bytes 14980
  49.9 20.9 %all-to-all-start.1 = ((f32[128,1,512]{2,1,0:T(1,128)}), f32[128,1,512]{2,1,0:T(1,128)S(1)}, u32[]{:S(2)}, u32[]{:S(2)}) async-start(f32[128,1,512]{2,1,0:T(1,128)} %copy.84), calls=%async_computation.1 | async-start | bytes 524288 | tf_op jit(solution)/shard_map/all_to_all | solution.py:66
  59.7 96.8 %reduce-scatter.2.cloned.1.call-start = ((), (), s32[]{:S(2)}) async-start(), calls=%async_computation.4 | async-start | bytes 2621440 | tf_op jit(solution)/shard_map/reduce_scatter | solution.py:88
  126.0 4.8 copy-start.5
  130.8 66.4 %all-gather.2.cloned.1.call-start = ((), (), s32[]{:S(2)}) async-start(), calls=%async_computation.5 | async-start | bytes 2621440 | tf_op jit(solution)/shard_map/all_gather | solution.py:104
  156.5 9.0 %copy-start.1 = (f32[128,8,128]{2,0,1:T(8,128)S(1)}, f32[128,8,128]{2,0,1:T(8,128)}, u32[]{:S(2)}) copy-start(f32[128,8,128]{2,0,1:T(8,128)} %reduce-scatter.2.cloned.1.call-done) | copy-start | bytes 1572868
  159.0 3.4 copy-start.8
  160.3 2.2 copy-start.16
  166.6 84.0 %all-reduce.6.cloned.1.call-start = ((), (), s32[]{:S(2)}) async-start(), calls=%async_computation.6 | async-start | bytes 2097152 | tf_op jit(solution)/shard_map/psum | solution.py:115
  202.6 3.4 copy-start.4
  204.5 2.7 copy-start.22
  204.6 3.7 copy-start.24
  206.0 229.3 %all-reduce.8.cloned.1.call-start = ((), (), s32[]{:S(2)}) async-start(), calls=%async_computation.7 | async-start | bytes 131072 | tf_op jit(solution)/shard_map/psum | solution.py:135
  210.1 4.4 copy-start.7
  210.1 291.5 %all-reduce.10.cloned.1.call-start = ((), (), s32[]{:S(2)}) async-start(), calls=%async_computation.8 | async-start | bytes 2621440 | tf_op jit(solution)/shard_map/psum | solution.py:134
  328.0 13.8 %copy-start.19 = (f32[13,96]{1,0:T(8,128)S(1)}, f32[13,96]{1,0:T(8,128)}, u32[]{:S(2)}) copy-start(f32[13,96]{1,0:T(8,128)} %param.13) | copy-start | bytes 14980
  330.2 83.0 %all-to-all-start.2 = ((f32[128,1,128]{2,1,0:T(1,128)}), f32[128,1,128]{2,1,0:T(1,128)S(1)}, u32[]{:S(2)}, u32[]{:S(2)}) async-start(f32[128,1,128]{2,1,0:T(1,128)} %bitcast.28), calls=%async_computation.3 | async-start | bytes 131072 | tf_op jit(solution)/shard_map/all_to_all | solution.py:129
  435.3 69.3 %copy-start.15 = (f32[2,128,64]{1,2,0:T(8,128)S(1)}, f32[2,128,64]{1,2,0:T(8,128)}, u32[]{:S(2)}) copy-start(f32[2,128,64]{1,2,0:T(8,128)} %all-reduce.8.cloned.1.call-done) | copy-start | bytes 196612
  501.6 2.3 copy-start.11
  (9 other events, 10.5 us)
Sparse Core Ops, SparseCore 0:
  131.0 25.5 reduce-scatter.1
  166.7 30.4 all-gather.1
  206.1 44.3 all-reduce.5
  255.1 140.0 all-reduce.7
  399.5 102.1 all-reduce.9
where the time goes:
time: 517 us; the launch traced here: 512 us
  waiting for transfers between devices  159 us (31%)
  local copies, waits for them, and re-layouts  109 us (21%)
  other arithmetic  92.2 us (18%)
  blocking collectives  68.5 us (13%)
  matrix products  35.5 us (7%)
  starting transfers between devices  32.9 us (6%)
  between operations  14.6 us (3%)
    scatter-add x1, other arithmetic, on_device(): jnp.zeros((owner_count * capacity, entry_width), jnp.float32).at[flat_slots]  71.9 us
    psum x1, blocking collectives, on_device(): lax.psum((dense_weight_grad, gate_grad, tower_grad, head_grad), ('batch',...  68.5 us
    psum x1, waiting for transfers between devices, on_device(): in_grad, out_grad = lax.psum((in_grad, out_grad), 'batch')  66.3 us
    gather x2, local copies, waits for them, and re-layouts, on_device(): jnp.take(fetched.reshape(owner_count * capacity, entry_width), flat_slots...  49.1 us
    psum x1, waiting for transfers between devices, on_device(): feature_grad = lax.psum(feature_part, 'hidden')  32.7 us
    all_gather x1, waiting for transfers between devices, on_device(): lax.all_gather(local_pre_grad, 'hidden', axis=0, tiled=True)  27.6 us
    unnamed x57, local copies, waits for them, and re-layouts  27.2 us
    reduce_scatter x1, waiting for transfers between devices, on_device(): lax.psum_scatter(jnp.einsum('nek,eko->neo', inner, expert_out, precision=...  23.8 us
  transfers between devices with their start and end apart: 8, of which 5 were waited for; matrix products, arithmetic and copies ran while one was open for 26% of the time, Pallas kernels for 0%

commit v1 on v0

v1 whole, which is shorter than its diff:
```python
import jax
import jax.numpy as jnp
from jax import lax
from jax.experimental import pallas as pl
from jax.experimental.pallas import tpu as pltpu
from jax.sharding import PartitionSpec as P

f32 = jnp.float32
bf16 = jnp.bfloat16
MESH = pl.DeviceIdType.MESH
VMEM = pl.BlockSpec(memory_space=pltpu.VMEM)
LIMIT = 56 * 2**20

TABLES, ROWS, ENTRY = 26, 1024, 16
BATCH, HIDDEN = 32, 4
DEVICES = BATCH * HIDDEN
EXPERTS, UNITS, OUT, WIDTH = 8, 64, 128, 512
TASKS, TOWER, DENSE, PROJ = 2, 64, 13, 96
EXAMPLES = 512
EMBED = TABLES * ENTRY

IN_ROWS, OUT_ROWS, GATE_ROWS, TOWER_ROWS = 2048, 512, 64, 128
OUT_AT = IN_ROWS
GATE_AT = OUT_AT + OUT_ROWS
TOWER_AT = GATE_AT + GATE_ROWS
DENSE_AT = TOWER_AT + TOWER_ROWS
HEAD_AT = DENSE_AT + 16
PIECE = 88
HALF = 16 * PIECE
SUMMED = 2 * HALF


def split(value):
    high = value.astype(bf16)
    return high, (value - high.astype(f32)).astype(bf16)


def dot_nn(a, b):
    return lax.dot_general(a, b, (((1,), (0,)), ((), ())), preferred_element_type=f32)


def dot_nt(a, b):
    return lax.dot_general(a, b, (((1,), (1,)), ((), ())), preferred_element_type=f32)


def dot3_nn(a, b):
    (ah, al), (bh, bl) = a, b
    return dot_nn(jnp.concatenate([ah, al, ah], 1), jnp.concatenate([bh, bh, bl], 0))


def dot3_nt(a, b):
    (ah, al), (bh, bl) = a, b
    return dot_nt(jnp.concatenate([ah, al, ah], 1), jnp.concatenate([bh, bh, bl], 1))


def sigmoid(value):
    return 0.5 * jnp.tanh(0.5 * value) + 0.5


def silu_both(value):
    sigma = sigmoid(value)
    result = value * sigma
    return result, sigma + result * (1.0 - sigma)


def iota(shape, axis):
    return lax.broadcasted_iota(jnp.int32, shape, axis)


def place():
    b, h = lax.axis_index("batch"), lax.axis_index("hidden")
    return b, h, lax.rem(b, 2)


def target(b, h):
    return {"batch": b, "hidden": h}


def remote(src, dst, send, recv, b, h):
    return pltpu.make_async_remote_copy(src, dst, send, recv, device_id=target(b, h), device_id_type=MESH)


def bulk_wait(ref, sem):
    pltpu.make_async_copy(ref, ref, sem).wait()


def ids_by_query(received):
    turned = jnp.concatenate([received] * 4, 0).T
    lane = iota((8, 128), 1) // 32
    out = jnp.zeros((8, 128), jnp.int32)
    for q in range(4):
        out = jnp.where(lane == q, turned[q * 8 : q * 8 + 8, :], out)
    return out


def fetch_kernel(
    req, tab, win, wout, cot,
    rows_out, ids_out, win_all, wout_all, cot_all,
    id_turned, id_send, id_recv, row_send, tab_split,
    y_send, y_recv, core_send, core_recv, cot_send, cot_recv, id_ssem, id_rsem, row_ssem, row_rsem, local_sem,
):
    b, h, core = place()
    sibling = b + 1 - 2 * core
    me = b * HIDDEN + h
    barrier = pltpu.get_barrier_semaphore()

    def greet(i, carry):
        other = lax.rem(me + i, DEVICES)
        pl.semaphore_signal(
            barrier, inc=1, device_id=target(other // HIDDEN, lax.rem(other, HIDDEN)), device_id_type=MESH
        )
        return carry

    lax.fori_loop(1, DEVICES, greet, 0)
    id_turned[...] = jnp.concatenate([req[...]] * 4, 0).T
    id_send[...] = id_turned[pl.ds(h, BATCH, stride=HIDDEN), :]
    pl.semaphore_wait(barrier, DEVICES - 1)

    def send_ids(i, carry):
        other = lax.rem(b + i, BATCH)
        remote(id_send.at[pl.ds(other, 1)], id_recv.at[pl.ds(b, 1)], id_ssem, id_rsem, other, h).start()
        return carry

    lax.fori_loop(1, BATCH, send_ids, 0)
    half = pl.ds(pl.multiple_of(core * 256, 256), 256)
    y_copies = []
    for i in range(1, HIDDEN):
        other = lax.rem(h + i, HIDDEN)
        y_copies.append(
            (
                remote(win.at[half], win_all.at[h, half], y_send.at[i - 1, 0], y_recv.at[i - 1, 0], b, other),
                remote(wout.at[half], wout_all.at[h, half], y_send.at[i - 1, 1], y_recv.at[i - 1, 1], b, other),
                remote(cot, cot_all.at[h], cot_send.at[i - 1], cot_recv.at[i - 1], b, other),
            )
        )
        for copy in y_copies[-1]:
            copy.start()
    own = (
        pltpu.make_async_copy(win, win_all.at[h], local_sem.at[0]),
        pltpu.make_async_copy(wout, wout_all.at[h], local_sem.at[1]),
        pltpu.make_async_copy(cot, cot_all.at[h], local_sem.at[2]),
    )
    for copy in own:
        copy.start()
    high, low = split(tab[...])
    tab_split[0:EMBED, :] = high
    tab_split[EMBED : 2 * EMBED, :] = low
    id_recv[pl.ds(b, 1), :] = id_send[pl.ds(b, 1), :]
    bulk_wait(id_recv.at[pl.ds(0, BATCH - 1)], id_rsem)
    ids = ids_by_query(id_recv[...])
    ids_out[...] = ids
    table, row = ids // ROWS, lax.rem(ids, ROWS)
    found = []
    for pair in range(4):
        hot = jnp.concatenate(
            [(iota((ROWS, 128), 0) == row[j : j + 1, :]).astype(f32).astype(bf16) for j in (2 * pair, 2 * pair + 1)], 1
        )
        got = dot_nn(tab_split[...], hot)
        for part in range(2):
            wanted = table[2 * pair + part : 2 * pair + part + 1, :]
            total = jnp.zeros((ENTRY, 128), f32)
            for t in range(TABLES):
                block = got[t * ENTRY : (t + 1) * ENTRY, part * 128 : part * 128 + 128]
                rest = got[EMBED + t * ENTRY : EMBED + (t + 1) * ENTRY, part * 128 : part * 128 + 128]
                total = jnp.where(wanted == t, block + rest, total)
            found.append(total)
    turned = jnp.concatenate(found, 0).T
    for q in range(4):
        row_send[pl.ds(q, BATCH, stride=4), :] = turned[q * 32 : q * 32 + 32, :]
    mine = pl.ds(me * 4, 4)

    def send_rows(i, carry):
        other = lax.rem(me + i, DEVICES)
        group = other // HIDDEN
        remote(
            row_send.at[pl.ds(group * 4, 4)], rows_out.at[mine], row_ssem, row_rsem, group, lax.rem(other, HIDDEN)
        ).start()
        return carry

    lax.fori_loop(1, DEVICES, send_rows, 0)
    rows_out[mine, :] = row_send[pl.ds(b * 4, 4), :]
    forwards = []
    for i in range(1, HIDDEN):
        source = lax.rem(h - i + HIDDEN, HIDDEN)
        for which, whole in ((0, win_all), (1, wout_all)):
            y_copies[i - 1][which].wait_recv()
            block = whole.at[source, half]
            forwards.append(
                remote(block, block, core_send.at[i - 1, which], core_recv.at[i - 1, which], sibling, h)
            )
            forwards[-1].start()
        y_copies[i - 1][2].wait_recv()
    bulk_wait(rows_out.at[pl.ds(0, (DEVICES - 1) * 4)], row_rsem)
    for copy in forwards:
        copy.wait()
    for copies in y_copies:
        for copy in copies:
            copy.wait_send()
    for copy in own:
        copy.wait()
    bulk_wait(id_send.at[pl.ds(0, BATCH - 1)], id_ssem)
    bulk_wait(rows_out.at[pl.ds(0, (DEVICES - 1) * 4)], row_ssem)


def hot_of(code, count):
    return (iota((count, code.shape[1]), 0) == code).astype(f32).astype(bf16)


def model_kernel(
    rows, slots, dense, dense_weight, win_all, wout_all, gate_weight, tower_weight, head, cot_all,
    pred_out, dense_grad_out, sums, message,
    wh, wl, wth, wtl, oh, ol, oth, otl,
    lists, feat_h, feat_l, dense_pad, weight_pad, head_pad,
    inner_h, inner_l, slope, ig_h, ig_l, eo, eslope, ep_h, ep_l, gates, gate_slope, mixed, mixed_grad, fg, slot_sum, slot_done,
):
    b, h, core = place()
    for e in range(EXPERTS):
        at = pl.ds(e * UNITS, UNITS)
        value = jnp.concatenate([win_all[i, at, :] for i in range(HIDDEN)], 0)
        wh[e], wl[e] = split(value)
        wth[e], wtl[e] = split(value.T)
        value = jnp.concatenate([wout_all[i, at, :] for i in range(HIDDEN)], 0)
        oh[e], ol[e] = split(value)
        oth[e], otl[e] = split(value.T)
    for q in range(4):
        high, low = split(rows[pl.ds(q, DEVICES, stride=4), :].T)
        lists[0:128, q * 128 : q * 128 + 128] = high
        lists[128:256, q * 128 : q * 128 + 128] = low

    def codes(t):
        slot = slots[pl.ds(t, 1), :]
        return (slot % 32) // 8 * 128 + slot // 32, slot % 8

    def gather(t, carry):
        code, low = codes(t)
        got = dot_nn(lists[...], hot_of(code, 512))
        high_sum = jnp.zeros((ENTRY, EXAMPLES), f32)
        low_sum = jnp.zeros((ENTRY, EXAMPLES), f32)
        for j in range(8):
            high_sum = jnp.where(low == j, got[j * 16 : j * 16 + 16, :], high_sum)
            low_sum = jnp.where(low == j, got[128 + j * 16 : 128 + j * 16 + 16, :], low_sum)
        at = pl.ds(pl.multiple_of(t * ENTRY, ENTRY), ENTRY)
        feat_h[at, :] = high_sum.astype(bf16)
        feat_l[at, :] = low_sum.astype(bf16)
        return carry

    lax.fori_loop(0, TABLES, gather, 0)
    dense_pad[...] = jnp.zeros_like(dense_pad)
    dense_pad[0:DENSE, :] = dense[...]
    weight_pad[...] = jnp.zeros_like(weight_pad)
    weight_pad[0:DENSE, 0:PROJ] = dense_weight[...]
    head_pad[...] = jnp.zeros_like(head_pad)
    head_pad[0:TASKS, 0:TOWER] = head[...]
    dense_split = split(dense_pad[...])
    projected = dot3_nn(split(weight_pad[...].T), dense_split)
    high, low = split(projected[0:PROJ, :])
    feat_h[EMBED:WIDTH, :] = high
    feat_l[EMBED:WIDTH, :] = low
    gate_split = split(gate_weight[...])
    logits = dot3_nn(gate_split, (feat_h[...], feat_l[...]))
    for k in range(TASKS):
        part = logits[k * 8 : k * 8 + 8, :]
        raised = jnp.exp(part - jnp.max(part, axis=0, keepdims=True))
        gates[k * 8 : k * 8 + 8, :] = raised / jnp.sum(raised, axis=0, keepdims=True)
    mixed[...] = jnp.zeros_like(mixed)

    def forward(e, carry):
        pre = dot3_nn((wh[e], wl[e]), (feat_h[...], feat_l[...]))
        inner, slope[e] = silu_both(pre)
        high, low = split(inner)
        inner_h[e], inner_l[e] = high, low
        outputs, eslope[e] = silu_both(dot3_nn((oth[e], otl[e]), (high, low)))
        eo[e] = outputs
        for k in range(TASKS):
            mixed[k] = mixed[k] + gates[pl.ds(k * 8 + e, 1), :] * outputs
        return carry

    lax.fori_loop(0, EXPERTS, forward, 0)
    head_turned = head_pad[...].T
    tower_turned = split(tower_weight[...].T)
    tower_grads, score_grads, tower_list = [], [], []
    for k in range(TASKS):
        at = slice(k * TOWER, (k + 1) * TOWER)
        mixed_split = split(mixed[k])
        towers, tower_slope = silu_both(dot3_nn(split(tower_weight[at, :]), mixed_split))
        column = jnp.broadcast_to(head_turned[0:TOWER, k : k + 1], (TOWER, EXAMPLES))
        predicted = sigmoid(jnp.sum(towers * column, axis=0, keepdims=True))
        mixed_grad[k, 0:1, :] = predicted
        pred_out[k : k + 1, :] = mixed_grad[k, 0:1, pl.ds(pl.multiple_of(h * 128, 128), 128)]
        cotangent = jnp.concatenate([cot_all[i, k : k + 1, :] for i in range(HIDDEN)], 1)
        score = cotangent * predicted * (1.0 - predicted)
        pre_grad = score * column * tower_slope
        sums[TOWER_AT + k * TOWER : TOWER_AT + (k + 1) * TOWER, :] = dot3_nt(split(pre_grad), mixed_split)
        tower_grads.append(pre_grad)
        score_grads.append(score)
        tower_list.append(towers)
    nothing = jnp.zeros((TOWER, EXAMPLES), f32)
    mixed_grad[0] = dot3_nn(tower_turned, split(jnp.concatenate([tower_grads[0], nothing], 0)))
    mixed_grad[1] = dot3_nn(tower_turned, split(jnp.concatenate([nothing, tower_grads[1]], 0)))
    scores = jnp.concatenate(score_grads + [jnp.zeros((14, EXAMPLES), f32)], 0)
    head_rows = dot3_nt(split(scores), split(jnp.concatenate(tower_list, 0)))
    sums[HEAD_AT:SUMMED, :] = jnp.zeros((SUMMED - HEAD_AT, 128), f32)
    sums[HEAD_AT : HEAD_AT + 1, :] = jnp.where(iota((1, 128), 1) < TOWER, head_rows[0:1, :], head_rows[1:2, :])
    fg[...] = jnp.zeros_like(fg)
    mine = pl.ds(pl.multiple_of(h * UNITS, UNITS), UNITS)

    def backward(e, carry):
        outputs = eo[e]
        total = jnp.zeros((OUT, EXAMPLES), f32)
        for k in range(TASKS):
            grad = mixed_grad[k]
            gate_slope[pl.ds(k * 8 + e, 1), :] = jnp.sum(grad * outputs, axis=0, keepdims=True)
            total = total + gates[pl.ds(k * 8 + e, 1), :] * grad
        high, low = split(total * eslope[e])
        ep_h[e], ep_l[e] = high, low
        inner_grad = dot3_nn((oh[e], ol[e]), (high, low)) * slope[e]
        ig = split(inner_grad)
        ig_h[e], ig_l[e] = ig
        fg[...] += dot3_nn((wth[e], wtl[e]), ig)
        own = (inner_h[e, mine, :], inner_l[e, mine, :])
        sums[pl.ds(pl.multiple_of(OUT_AT + e * UNITS, UNITS), UNITS), :] = dot3_nt(own, (high, low))
        return carry

    lax.fori_loop(0, EXPERTS, backward, 0)
    feat = (feat_h[...], feat_l[...])
    own = tuple(jnp.concatenate([ref[e, mine, :] for e in range(EXPERTS)], 0) for ref in (ig_h, ig_l))
    in_grad = dot3_nt(own, feat)
    for q in range(4):
        sums[q * 512 : (q + 1) * 512, :] = in_grad[:, q * 128 : (q + 1) * 128]
    logit_grads = []
    for k in range(TASKS):
        gate, slopes = gates[k * 8 : k * 8 + 8, :], gate_slope[k * 8 : k * 8 + 8, :]
        logit_grads.append(gate * (slopes - jnp.sum(gate * slopes, axis=0, keepdims=True)))
    lgh, lgl = split(jnp.concatenate(logit_grads, 0))
    gate_grad = dot3_nt((lgh, lgl), feat)
    for q in range(4):
        sums[GATE_AT + q * 16 : GATE_AT + q * 16 + 16, :] = gate_grad[:, q * 128 : (q + 1) * 128]
    gh, gl = (part.astype(f32) for part in gate_split)
    stacked = jnp.concatenate([gh, gl, gh, jnp.zeros((80, WIDTH), f32)], 0).T.astype(bf16)
    fg[...] += dot_nn(stacked, jnp.concatenate([lgh, lgh, lgl, jnp.zeros((80, EXAMPLES), bf16)], 0))
    projected_grad = split(jnp.concatenate([fg[EMBED:WIDTH, :], jnp.zeros((32, EXAMPLES), f32)], 0))
    dense_grad_out[...] = dot3_nn(split(weight_pad[...]), projected_grad)[0:DENSE, :]
    sums[DENSE_AT : DENSE_AT + 16, :] = dot3_nt(dense_split, projected_grad)[0:16, :]
    slot_sum[...] = jnp.zeros_like(slot_sum)

    def scatter(t, carry):
        code, low = codes(t)
        grad = fg[pl.ds(pl.multiple_of(t * ENTRY, ENTRY), ENTRY), :]
        high = grad.astype(bf16).astype(f32)
        rest = grad - high
        parts = [jnp.where(low == j, part, 0.0) for part in (high, rest) for j in range(8)]
        spread = jnp.concatenate(parts, 0).astype(bf16)
        slot_sum[...] += dot_nt(hot_of(code, 512), spread)
        return carry

    lax.fori_loop(0, TABLES, scatter, 0)
    slot_done[...] = slot_sum[:, 0:128] + slot_sum[:, 128:256]
    for q in range(4):
        message[pl.ds(q, BATCH, stride=4), :] = slot_done[pl.ds(q * 128 + h, BATCH, stride=HIDDEN), :]


def sum_kernel(
    sums, message, ids,
    table_grad, total,
    got, from_core, reduced, pieces,
    core_send, core_recv, slot_ssem, slot_rsem, piece_ssem, piece_rsem, full_ssem, full_rsem,
):
    b, h, core = place()
    sibling = b + 1 - 2 * core
    chip = b // 2
    barrier = pltpu.get_barrier_semaphore()

    def greet(i, carry):
        pl.semaphore_signal(barrier, inc=1, device_id=target(lax.rem(b + i, BATCH), h), device_id_type=MESH)
        return carry

    lax.fori_loop(1, BATCH, greet, 0)
    pl.semaphore_wait(barrier, BATCH - 1)
    mine = pl.ds(pl.multiple_of(core * HALF, HALF), HALF)
    theirs = pl.ds(pl.multiple_of((1 - core) * HALF, HALF), HALF)
    exchange = remote(sums.at[theirs], from_core, core_send.at[0], core_recv.at[0], sibling, h)
    exchange.start()

    def send_slots(i, carry):
        other = lax.rem(b + i, BATCH)
        remote(message.at[pl.ds(other * 4, 4)], got.at[pl.ds(b * 4, 4)], slot_ssem, slot_rsem, other, h).start()
        return carry

    lax.fori_loop(1, BATCH, send_slots, 0)
    got[pl.ds(b * 4, 4), :] = message[pl.ds(b * 4, 4), :]
    exchange.wait()
    reduced[...] = sums[mine, :] + from_core[...]

    def send_pieces(i, carry):
        other = lax.rem(chip + i, 16)
        remote(
            reduced.at[pl.ds(pl.multiple_of(other * PIECE, 8), PIECE)],
            pieces.at[pl.ds(pl.multiple_of(chip * PIECE, 8), PIECE)],
            piece_ssem, piece_rsem, other * 2 + core, h,
        ).start()
        return carry

    lax.fori_loop(1, 16, send_pieces, 0)
    own = pl.ds(pl.multiple_of(chip * PIECE, 8), PIECE)
    pieces[own, :] = reduced[own, :]
    bulk_wait(got.at[pl.ds(0, (BATCH - 1) * 4)], slot_rsem)
    turned = jnp.concatenate([got[pl.ds(q, BATCH, stride=4), :] for q in range(4)], 0).T
    table, row = ids[...] // ROWS, lax.rem(ids[...], ROWS)
    high = turned.astype(bf16).astype(f32)
    rest = turned - high
    spread = []
    for j in range(8):
        parts = [
            jnp.where(table[j : j + 1, :] == t, part[j * 16 : j * 16 + 16, :], 0.0)
            for part in (high, rest)
            for t in range(TABLES)
        ]
        spread.append(jnp.concatenate(parts, 0).astype(bf16))
    spread = jnp.concatenate(spread, 1)
    for part in range(4):
        hot = jnp.concatenate(
            [(iota((256, 128), 0) + part * 256 == row[j : j + 1, :]).astype(f32).astype(bf16) for j in range(8)], 1
        )
        both = dot_nt(spread, hot)
        table_grad[:, part * 256 : (part + 1) * 256] = both[0:EMBED, :] + both[EMBED : 2 * EMBED, :]
    bulk_wait(pieces.at[pl.ds(0, 15 * PIECE)], piece_rsem)
    bulk_wait(pieces.at[pl.ds(0, 15 * PIECE)], piece_ssem)
    value = pieces[0:PIECE, :]
    for i in range(1, 16):
        value = value + pieces[i * PIECE : (i + 1) * PIECE, :]
    place_of = pl.ds(pl.multiple_of(core * HALF + chip * PIECE, 8), PIECE)
    total[place_of, :] = value

    def send_full(i, carry):
        other = lax.rem(chip + i, 16)
        remote(total.at[place_of], total.at[place_of], full_ssem, full_rsem, other * 2 + core, h).start()
        return carry

    lax.fori_loop(1, 16, send_full, 0)
    bulk_wait(total.at[pl.ds(0, 15 * PIECE)], full_rsem)
    last = remote(total.at[mine], total.at[mine], core_send.at[1], core_recv.at[1], sibling, h)
    last.start()
    last.wait()
    bulk_wait(total.at[pl.ds(0, 15 * PIECE)], full_ssem)
    bulk_wait(message.at[pl.ds(0, (BATCH - 1) * 4)], slot_ssem)


def call(kernel, outs, ins, scratch, name, collective_id=None):
    params = dict(vmem_limit_bytes=LIMIT)
    if collective_id is not None:
        params.update(collective_id=collective_id, has_side_effects=True)
    return pl.pallas_call(
        kernel,
        out_shape=[jax.ShapeDtypeStruct(shape, dtype) for shape, dtype in outs],
        in_specs=[VMEM] * ins,
        out_specs=[VMEM] * len(outs),
        scratch_shapes=scratch,
        compiler_params=pltpu.CompilerParams(**params),
        name=name,
    )


def on_device(
    tables, dense, dense_weight, expert_in, expert_out, gate_weight, tower_weight, head_weight, slots, requests, pred_cot
):
    i32 = jnp.int32
    dma = pltpu.SemaphoreType.DMA
    req = requests[0].T
    tab = tables.transpose(0, 2, 1).reshape(EMBED, ROWS)
    win = expert_in.transpose(1, 2, 0).reshape(EXPERTS * UNITS, WIDTH)
    wout = expert_out.reshape(EXPERTS * UNITS, OUT)
    gate = gate_weight.transpose(0, 2, 1).reshape(TASKS * EXPERTS, WIDTH)
    tower = tower_weight.transpose(0, 2, 1).reshape(TASKS * TOWER, OUT)
    rows, ids, win_all, wout_all, cot_all = call(
        fetch_kernel,
        [
            ((512, 128), f32), ((8, 128), i32), ((HIDDEN, 512, WIDTH), f32), ((HIDDEN, 512, OUT), f32),
            ((HIDDEN, TASKS, 128), f32),
        ],
        5,
        [
            pltpu.VMEM((128, 128), i32), pltpu.VMEM((32, 128), i32), pltpu.VMEM((32, 128), i32),
            pltpu.VMEM((128, 128), f32), pltpu.VMEM((2 * EMBED, ROWS), bf16),
            dma((3, 2)), dma((3, 2)), dma((3, 2)), dma((3, 2)), dma((3,)), dma((3,)), dma, dma, dma, dma, dma((3,)),
        ],
        "fetch",
        0,
    )(req, tab, win, wout, pred_cot.T)
    units = EXPERTS, 256, EXAMPLES
    outputs = EXPERTS, OUT, EXAMPLES
    predictions, dense_grad, sums, message = call(
        model_kernel,
        [((TASKS, 128), f32), ((DENSE, EXAMPLES), f32), ((SUMMED, 128), f32), ((128, 128), f32)],
        10,
        [
            pltpu.VMEM((EXPERTS, 256, WIDTH), bf16), pltpu.VMEM((EXPERTS, 256, WIDTH), bf16),
            pltpu.VMEM((EXPERTS, WIDTH, 256), bf16), pltpu.VMEM((EXPERTS, WIDTH, 256), bf16),
            pltpu.VMEM((EXPERTS, 256, OUT), bf16), pltpu.VMEM((EXPERTS, 256, OUT), bf16),
            pltpu.VMEM((EXPERTS, OUT, 256), bf16), pltpu.VMEM((EXPERTS, OUT, 256), bf16),
            pltpu.VMEM((256, 512), bf16), pltpu.VMEM((WIDTH, EXAMPLES), bf16), pltpu.VMEM((WIDTH, EXAMPLES), bf16),
            pltpu.VMEM((128, EXAMPLES), f32), pltpu.VMEM((128, 128), f32), pltpu.VMEM((128, 128), f32),
            pltpu.VMEM(units, bf16), pltpu.VMEM(units, bf16), pltpu.VMEM(units, f32),
            pltpu.VMEM(units, bf16), pltpu.VMEM(units, bf16),
            pltpu.VMEM(outputs, f32), pltpu.VMEM(outputs, f32), pltpu.VMEM(outputs, bf16), pltpu.VMEM(outputs, bf16),
            pltpu.VMEM((16, EXAMPLES), f32), pltpu.VMEM((16, EXAMPLES), f32),
            pltpu.VMEM((TASKS, OUT, EXAMPLES), f32), pltpu.VMEM((TASKS, OUT, EXAMPLES), f32),
            pltpu.VMEM((WIDTH, EXAMPLES), f32), pltpu.VMEM((512, 256), f32), pltpu.VMEM((512, 128), f32),
        ],
        "model",
    )(rows, slots.T, dense.T, dense_weight, win_all, wout_all, gate, tower, head_weight, cot_all)
    table_grad, total = call(
        sum_kernel,
        [((EMBED, ROWS), f32), ((SUMMED, 128), f32)],
        3,
        [
            pltpu.VMEM((128, 128), f32), pltpu.VMEM((HALF, 128), f32), pltpu.VMEM((HALF, 128), f32),
            pltpu.VMEM((HALF, 128), f32),
            dma((2,)), dma((2,)), dma, dma, dma, dma, dma, dma,
        ],
        "sum",
        1,
    )(sums, message, ids)
    in_grad = total[:IN_ROWS].reshape(4, EXPERTS, UNITS, 128).transpose(0, 3, 1, 2).reshape(WIDTH, EXPERTS, UNITS)
    out_grad = total[OUT_AT:GATE_AT].reshape(EXPERTS, UNITS, OUT)
    gate_grad = total[GATE_AT:TOWER_AT].reshape(4, TASKS, EXPERTS, 128).transpose(1, 0, 3, 2)
    tower_grad = total[TOWER_AT:DENSE_AT].reshape(TASKS, TOWER, OUT).transpose(0, 2, 1)
    return (
        predictions.T,
        dense_grad.T,
        table_grad.reshape(TABLES, ENTRY, ROWS).transpose(0, 2, 1),
        total[DENSE_AT : DENSE_AT + DENSE, :PROJ],
        in_grad,
        out_grad,
        gate_grad.reshape(TASKS, WIDTH, EXPERTS),
        tower_grad,
        total[HEAD_AT].reshape(TASKS, TOWER),
    )


def solution(mesh):
    placed = (
        P(None, ("batch", "hidden"), None),
        P("batch", None),
        P(),
        P(None, None, "hidden"),
        P(None, "hidden", None),
        P(),
        P(),
        P(),
        P("batch", None),
        P("batch", None, None),
        P(("batch", "hidden"), None),
    )
    return jax.shard_map(
        on_device,
        mesh=mesh,
        in_specs=placed,
        out_specs=(
            P(("batch", "hidden"), None),
            P("batch", None),
            P(None, ("batch", "hidden"), None),
            P(),
            P(None, None, "hidden"),
            P(None, "hidden", None),
            P(),
            P(),
            P(),
        ),
        check_vma=False,
    )
```

time: 517 us -> 137 us (0.26)
  waiting for transfers between devices: 159 us -> 0 us
  Pallas kernels: 0 us -> 125 us
  local copies, waits for them, and re-layouts: 109 us -> 10.9 us
  other arithmetic: 92.2 us -> 0 us
  blocking collectives: 68.5 us -> 0 us
  matrix products: 35.5 us -> 0 us
  starting transfers between devices: 32.9 us -> 0 us
  between operations: 14.6 us -> 0.67 us
    pallas_call x0 -> x3, Pallas kernels: none -> 125 us  [the longest x1 50.7 us: on_device(): call(fetch_kernel, [((512, 128), f32), ((8, 128), i32), ((HIDDEN, 512, WI...]
    psum x3 -> x0, waiting for transfers between devices: 99 us -> none  [the longest x1 66.3 us: on_device(): in_grad, out_grad = lax.psum((in_grad, out_grad), 'batch')]
    scatter-add x2 -> x0, other arithmetic: 83.6 us -> none  [the longest x1 71.9 us: on_device(): jnp.zeros((owner_count * capacity, entry_width), jnp.float32).at[flat_slots]]
    psum x1 -> x0, blocking collectives: 68.5 us -> none  [on_device(): lax.psum((dense_weight_grad, gate_grad, tower_grad, head_grad), ('batch',...]
    gather x7 -> x0, local copies, waits for them, and re-layouts: 67 us -> none  [the longest x2 49.1 us: on_device(): jnp.take(fetched.reshape(owner_count * capacity, entry_width), flat_slots...]
    dot_general x19 -> x0, matrix products: 35.2 us -> none  [the longest x1 4.78 us: on_device(): jnp.einsum('nek,eko->neo', inner, expert_out, precision=highest)]
    all_to_all x3 -> x0, starting transfers between devices: 31.8 us -> none  [the longest x1 11.5 us: on_device(): lax.all_to_all(asked, ('batch', 'hidden'), split_axis=0, concat_axis=0, t...]
    all_gather x1 -> x0, waiting for transfers between devices: 27.6 us -> none  [on_device(): lax.all_gather(local_pre_grad, 'hidden', axis=0, tiled=True)]
  transfers between devices with their start and end apart: 8 -> 0, of which waited for: 5 -> 0; matrix products, arithmetic and copies ran while one was open for 26% -> 0% of each run, Pallas kernels for 0% -> 0%
where the time goes in v1:
time: 137 us
  Pallas kernels  125 us (91%)
  local copies, waits for them, and re-layouts  10.9 us (8%)
    pallas_call x1, Pallas kernels, on_device(): call(fetch_kernel, [((512, 128), f32), ((8, 128), i32), ((HIDDEN, 512, WI...  50.7 us
    pallas_call x1, Pallas kernels, on_device(): call(model_kernel, [((TASKS, 128), f32), ((DENSE, EXAMPLES), f32), ((SUMM...  42.3 us
    pallas_call x1, Pallas kernels, on_device(): call(sum_kernel, [((EMBED, ROWS), f32), ((SUMMED, 128), f32)], 3, [pltpu....  32.1 us

profile of v1, /device:TPU:1, one launch (start us, length us, event | category | flops | bytes accessed | tf_op | source)
XLA Modules:
  0.0 136.6 jit_solution(4494312203224336354)
XLA Ops:
  0.6 50.7 %fetch.1 = (f32[512,128]{1,0:T(8,128)}, s32[8,128]{1,0:T(8,128)}, f32[4,512,512]{2,1,0:T(8,128)}, f32[4,512,128]{2,1,0:T(8,128)}, f32[4,2,128]{2,1,0:T(2,128)}) custom-call(s32[32,128]{1,0:T(8,128)} %bitcast.55, f32[416,1024]{1,0:T(8,128)} %bitcast.42, f32[512,512]{1,0:T(8,128)} %bitcast.44, f32[512,128]{1,0:T(8,128)} %bitcast.47, f32[2,128]{1,0:T(2,128)} %bitcast.56), custom_call_target="tpu_custom_call" | custom-call | tf_op jit(solution)/shard_map/fetch/pallas_call | solution.py:474
  51.3 42.3 %model.1 = (f32[2,128]{1,0:T(2,128)}, f32[13,512]{1,0:T(8,128)}, f32[2816,128]{1,0:T(8,128)}, f32[128,128]{1,0:T(8,128)}) custom-call(f32[512,128]{1,0:T(8,128)} %get-tuple-element.20.rows, s32[26,512]{1,0:T(8,128)} %bitcast.49, f32[13,512]{1,0:T(8,128)} %bitcast.52, f32[13,96]{1,0:T(8,128)} %dense_weight.1, f32[4,512,512]{2,1,0:T(8,128)} %get-tuple-element.21.win_all, ...), custom_call_target="tpu_custom_call" | custom-call | tf_op jit(solution)/shard_map/model/pallas_call | solution.py:491
  93.6 32.1 %sum.1 = (f32[416,1024]{1,0:T(8,128)}, f32[2816,128]{1,0:T(8,128)}) custom-call(f32[2816,128]{1,0:T(8,128)} %get-tuple-element.26.sums, f32[128,128]{1,0:T(8,128)} %get-tuple-element.27.message, s32[8,128]{1,0:T(8,128)} %get-tuple-element.28.ids), custom_call_target="tpu_custom_call" | custom-call | tf_op jit(solution)/shard_map/sum/pallas_call | solution.py:511
  125.7 0.7 slice_reduce_fusion
  126.4 0.6 reshape_squeeze.3
  127.1 1.3 slice.18
  128.4 0.8 slice.21
  129.1 0.6 copy.26
  129.7 1.5 %slice.22 = f32[128,128]{1,0:T(8,128)} slice(f32[2816,128]{1,0:T(8,128)} %get-tuple-element.30), slice={[2624:2752], [0:128]} | slice | bytes 131072 | tf_op jit(solution)/shard_map/slice | solution.py:526
  131.2 1.7 %slice.20 = f32[512,128]{1,0:T(8,128)} slice(f32[2816,128]{1,0:T(8,128)} %get-tuple-element.30), slice={[2048:2560], [0:128]} | slice | bytes 524288 | tf_op jit(solution)/shard_map/slice | solution.py:524
  132.9 0.0 copy-start
  132.9 1.4 %slice.19 = f32[2048,128]{1,0:T(8,128)S(1)} slice(f32[2816,128]{1,0:T(8,128)} %get-tuple-element.30), slice={[0:2048], [0:128]} | slice | bytes 2097152 | tf_op jit(solution)/shard_map/slice | solution.py:523
  134.3 1.1 copy.25
  135.4 0.0 copy-done
  135.4 1.2 copy.28
Async XLA Ops:
  132.9 2.5 %copy-start = (f32[416,1024]{1,0:T(8,128)S(1)}, f32[416,1024]{1,0:T(8,128)}, u32[]{:S(2)}) copy-start(f32[416,1024]{1,0:T(8,128)} %get-tuple-element.29) | copy-start | bytes 5111812
